TPU v7x, 32 devices: a whole 2x2x4 slice. The times are simulated.
32 devices in a mesh: blk: 16 (over z, y, core), fld: 2 (over x).
Axes of the slice: x: 2, y: 2, z: 4, core: 2. Of those that a mesh axis runs over, the one named last changes fastest.
Arguments:
- vectors: bfloat16 [1024, 16384], P('blk', 'fld'), may hold values from -1.1953125 to 1.1953125
- norms: bfloat16 [1024], P('blk'), may hold values from 0.5 to 2
- offsets: int32 [2], replicated, may hold values from 1 to 7
- pivot_block: int32 [2, 3], replicated, may hold values from 0 to 15
- pivot_row: int32 [2, 3], replicated, may hold values from 0 to 63
Outputs:
- similarity: bfloat16 [2, 3, 1024, 64], P(None, None, ('blk', 'fld'))
All inputs are finite; a program needn't handle non-finite values.
Results may differ from a plain program's by a relative error of at most 0.014.
Values may be sent and summed in bfloat16 or wider, within the bound.
A program may use at most 64 MiB of HBM per device.

v0:
```python
import jax
import jax.numpy as jnp
from jax import lax
from jax.sharding import PartitionSpec as P

NOFF = 2


def from_behind(value, axis, by):
    peers = lax.axis_size(axis)
    return lax.ppermute(value, axis, [(i, (i + by) % peers) for i in range(peers)])


def body(vectors, norms, offsets, pivot_block, pivot_row):
    rows = vectors.shape[0]
    blocks = lax.axis_size("blk")
    mine = lax.axis_index("blk")
    slices = lax.axis_size("fld")
    place = lax.axis_index("fld")
    share = rows // slices
    levels = (blocks // 2 - 1).bit_length()
    count_piv = pivot_block.shape[1]
    steps = NOFF * count_piv
    found_blocks = []
    found_norms = []
    for turn in range(NOFF):
        cur_block, cur_norm = (vectors, norms)
        for level in range(levels):
            moved = from_behind((cur_block, cur_norm), "blk", -(1 << level))
            taken = offsets[turn] // (1 << level) % 2 == 1
            cur_block = jnp.where(taken, moved[0], cur_block)
            cur_norm = jnp.where(taken, moved[1], cur_norm)
        found_blocks.append(cur_block)
        found_norms.append(cur_norm)
    partners = jnp.stack(found_blocks)
    partner_norms = jnp.stack(found_norms)
    flat_block = pivot_block.reshape(-1)
    flat_row = pivot_row.reshape(-1)
    picked = vectors[flat_row].astype(jnp.float32)
    picked_norms = norms[flat_row].astype(jnp.float32)
    owned = flat_block == mine
    summed = lax.psum(
        (jnp.where(owned[:, None], picked, 0.0), jnp.where(owned, picked_norms, 0.0)), "blk"
    )
    pivot_table = summed[0].astype(jnp.bfloat16)
    pivot_norm_table = summed[1]

    def tile(step):
        turn = step // count_piv
        pivot = pivot_table[step]
        pivot_norm = pivot_norm_table[step]
        partner = lax.dynamic_index_in_dim(partners, turn, 0, keepdims=False)
        scaled = (vectors.astype(jnp.float32) * pivot.astype(jnp.float32)[None, :]).astype(
            jnp.bfloat16
        )
        partial_value = lax.dot_general(
            scaled, partner, (((1,), (1,)), ((), ())), preferred_element_type=jnp.float32
        )
        return (partial_value.astype(jnp.bfloat16), pivot_norm)

    step_ids = jnp.arange(steps, dtype=jnp.int32)

    def step_each(carry, step):
        partial_value, pivot_norm = tile(step)
        summed_rows = lax.psum_scatter(
            partial_value, "fld", scatter_dimension=0, tiled=True
        ).astype(jnp.float32)
        return (carry, (summed_rows, pivot_norm))

    _, (field_sum, pivot_norms) = lax.scan(step_each, jnp.zeros((), jnp.float32), step_ids)
    own_norms = lax.dynamic_slice_in_dim(norms, place * share, share, 0).astype(jnp.float32)
    step_partner_norms = jnp.repeat(partner_norms.astype(jnp.float32), count_piv, axis=0)
    denominator = (
        own_norms[None, :, None] * pivot_norms[:, None, None] * step_partner_norms[:, None, :]
    )
    result = (field_sum / denominator).astype(jnp.bfloat16)
    return result.reshape(NOFF, count_piv, share, rows)


def solution(mesh):
    return jax.shard_map(
        body,
        mesh=mesh,
        in_specs=(P("blk", "fld"), P("blk"), P(), P(), P()),
        out_specs=P(None, None, ("blk", "fld"), None),
        check_vma=False,
    )
```

profile of v0, /device:TPU:5, one launch (start us, length us, event | category | flops | bytes accessed | tf_op | source)
XLA Modules:
  0.0 290.1 jit_solution(14202489317488943778)
XLA Ops:
  6.5 0.7 collective-permute-start
  7.2 0.7 broadcast_compare_fusion
  8.0 0.8 reshape.75
  8.8 2.1 gather_fusion
  10.9 1.3 fusion.7
  17.5 0.6 gather_fusion.1
  18.2 55.6 %all-reduce.2 = (bf16[6,8192]{1,0:T(8,128)(2,1)S(1)}, f32[6]{0:T(128)S(1)}) all-reduce(f32[6,8192]{1,0:T(8,128)S(1)} %convert_select_fusion, f32[6]{0:T(128)S(1)} %convert_select_fusion.1), channel_id=1, replica_groups=mesh['blk'=16,'fld'=2] {'blk'}, use_global_device_ids=true, to_apply=%region_0.1 | all-reduce | flops 49158 | bytes 294960 | tf_op jit(solution)/shard_map/psum | solution.py:42
  73.9 1.5 broadcast_select_fusion.2
  75.4 4.9 %collective-permute-start.1 = (bf16[64,8192]{1,0:T(8,128)(2,1)S(1)}, bf16[64,8192]{1,0:T(8,128)(2,1)}, u32[]{:S(2)}, u32[]{:S(2)}) collective-permute-start(bf16[64,8192]{1,0:T(8,128)(2,1)S(1)} %get-tuple-element.128), channel_id=1, source_target_pairs={{0,28},{2,30},{4,0},{6,2},{8,4},{10,6},{12,8},{14,10},{16,12},{18,... | collective-permute-start | bytes 3145736 | tf_op jit(solution)/shard_map/ppermute | solution.py:11
  80.3 4.7 %collective-permute-start.6 = (bf16[64]{0:T(256)(128)(2,1)S(1)}, bf16[64]{0:T(256)(128)(2,1)S(1)}, u32[]{:S(2)}, u32[]{:S(2)}) collective-permute-start(bf16[64]{0:T(256)(128)(2,1)S(1)} %get-tuple-element.130), channel_id=1, source_target_pairs={{0,28},{2,30},{4,0},{6,2},{8,4},{10,6},{12,8},{14,10},{16,12},{18,... | collective-permute-start | bytes 392 | tf_op jit(solution)/shard_map/ppermute | solution.py:11
  85.1 12.7 %collective-permute-done.6 = bf16[64]{0:T(256)(128)(2,1)S(1)} collective-permute-done((bf16[64]{0:T(256)(128)(2,1)S(1)}, bf16[64]{0:T(256)(128)(2,1)S(1)}, u32[]{:S(2)}, u32[]{:S(2)}) %collective-permute-start.6) | collective-permute-done | bytes 160 | tf_op jit(solution)/shard_map/ppermute | solution.py:11
  97.8 13.3 %collective-permute-start.7 = (bf16[64]{0:T(256)(128)(2,1)S(1)}, bf16[64]{0:T(256)(128)(2,1)S(1)}, u32[]{:S(2)}, u32[]{:S(2)}) collective-permute-start(bf16[64]{0:T(256)(128)(2,1)S(1)} %broadcast_select_fusion.8), channel_id=1, source_target_pairs={{0,24},{2,26},{4,28},{6,30},{8,0},{10,2},{12,4},{14,6},{16,8},{18,... | collective-permute-start | bytes 392 | tf_op jit(solution)/shard_map/ppermute | solution.py:11
  111.2 0.6 collective-permute-done.7
  111.8 1.7 collective-permute-done.9
  113.8 2.0 collective-permute-start.2
  115.8 20.9 %collective-permute-done.3 = bf16[64,8192]{1,0:T(8,128)(2,1)S(1)} collective-permute-done((bf16[64,8192]{1,0:T(8,128)(2,1)S(1)}, bf16[64,8192]{1,0:T(8,128)(2,1)S(1)}, u32[]{:S(2)}, u32[]{:S(2)}) %collective-permute-start.3) | collective-permute-done | bytes 1048608 | tf_op jit(solution)/shard_map/ppermute | solution.py:11
  136.8 4.0 %collective-permute-start.4 = (bf16[64,8192]{1,0:T(8,128)(2,1)S(1)}, bf16[64,8192]{1,0:T(8,128)(2,1)S(1)}, u32[]{:S(2)}, u32[]{:S(2)}) collective-permute-start(bf16[64,8192]{1,0:T(8,128)(2,1)S(1)} %broadcast_select_fusion.1), channel_id=1, source_target_pairs={{0,24},{2,26},{4,28},{6,30},{8,0},{10,2},{12,4},{14,6},{16,8},{18,... | collective-permute-start | bytes 3145736 | tf_op jit(solution)/shard_map/ppermute | solution.py:11
  141.0 16.4 %collective-permute-done.4 = bf16[64,8192]{1,0:T(8,128)(2,1)S(1)} collective-permute-done((bf16[64,8192]{1,0:T(8,128)(2,1)S(1)}, bf16[64,8192]{1,0:T(8,128)(2,1)S(1)}, u32[]{:S(2)}, u32[]{:S(2)}) %collective-permute-start.4) | collective-permute-done | bytes 1048608 | tf_op jit(solution)/shard_map/ppermute | solution.py:11
  157.5 0.2 pad_maximum_fusion
  157.7 124.8 %while.15 = (s32[]{:T(128)}, f32[6,32,64]{2,1,0:T(8,128)S(1)}, f32[6]{0:T(128)S(1)}, bf16[64,8192]{1,0:T(8,128)(2,1)S(1)}, s32[6]{0:T(128)S(1)}, /*index=5*/bf16...) while((s32[]{:T(128)}, f32[6,32,64]{2,1,0:T(8,128)S(1)}, f32[6]{0:T(128)S(1)}, ...), condition=%wide.region_4.5_spmd.clone, body=%wide.region_2.4_spmd.sunk.clone | while | flops 68696080 | bytes 2257743 | solution.py:70
  157.8 0.6 dynamic_slice.48
  162.3 1.1 convolution_convert_fusion.3
  163.4 0.2 dynamic-slice_dynamic-update-slice_fusion.3
  163.5 37.0 %reduce-scatter.2.cloned.1.call-done = bf16[32,64]{1,0:T(8,128)(2,1)} async-done(((bf16[64,64]{1,0:T(8,128)(2,1)}), bf16[32,64]{1,0:T(8,128)(2,1)}) %reduce-scatter.2.cloned.1.call-update) | async-done | bytes 4112 | tf_op jit(solution)/shard_map/while/body/eval_jaxpr/reduce_scatter | solution.py:65
  200.5 0.7 convert_dynamic-update-slice_fusion.3
  201.2 0.6 dynamic_slice.48
  205.7 1.1 convolution_convert_fusion.3
  206.8 0.2 dynamic-slice_dynamic-update-slice_fusion.3
  207.0 9.8 %reduce-scatter.2.cloned.1.call-done = bf16[32,64]{1,0:T(8,128)(2,1)} async-done(((bf16[64,64]{1,0:T(8,128)(2,1)}), bf16[32,64]{1,0:T(8,128)(2,1)}) %reduce-scatter.2.cloned.1.call-update) | async-done | bytes 4112 | tf_op jit(solution)/shard_map/while/body/eval_jaxpr/reduce_scatter | solution.py:65
  216.8 0.7 convert_dynamic-update-slice_fusion.3
  217.5 0.6 dynamic_slice.48
  222.0 1.1 convolution_convert_fusion.3
  223.1 0.2 dynamic-slice_dynamic-update-slice_fusion.3
  223.2 9.8 %reduce-scatter.2.cloned.1.call-done = bf16[32,64]{1,0:T(8,128)(2,1)} async-done(((bf16[64,64]{1,0:T(8,128)(2,1)}), bf16[32,64]{1,0:T(8,128)(2,1)}) %reduce-scatter.2.cloned.1.call-update) | async-done | bytes 4112 | tf_op jit(solution)/shard_map/while/body/eval_jaxpr/reduce_scatter | solution.py:65
  233.0 0.7 convert_dynamic-update-slice_fusion.3
  233.7 0.6 dynamic_slice.48
  238.2 1.1 convolution_convert_fusion.3
  239.5 9.8 %reduce-scatter.2.cloned.1.call-done = bf16[32,64]{1,0:T(8,128)(2,1)} async-done(((bf16[64,64]{1,0:T(8,128)(2,1)}), bf16[32,64]{1,0:T(8,128)(2,1)}) %reduce-scatter.2.cloned.1.call-update) | async-done | bytes 4112 | tf_op jit(solution)/shard_map/while/body/eval_jaxpr/reduce_scatter | solution.py:65
  249.2 0.7 convert_dynamic-update-slice_fusion.3
  249.9 0.6 dynamic_slice.48
  254.5 1.1 convolution_convert_fusion.3
  255.7 9.8 %reduce-scatter.2.cloned.1.call-done = bf16[32,64]{1,0:T(8,128)(2,1)} async-done(((bf16[64,64]{1,0:T(8,128)(2,1)}), bf16[32,64]{1,0:T(8,128)(2,1)}) %reduce-scatter.2.cloned.1.call-update) | async-done | bytes 4112 | tf_op jit(solution)/shard_map/while/body/eval_jaxpr/reduce_scatter | solution.py:65
  265.5 0.7 convert_dynamic-update-slice_fusion.3
  266.2 0.6 dynamic_slice.48
  270.7 1.0 convolution_convert_fusion.3
  272.0 9.8 %reduce-scatter.2.cloned.1.call-done = bf16[32,64]{1,0:T(8,128)(2,1)} async-done(((bf16[64,64]{1,0:T(8,128)(2,1)}), bf16[32,64]{1,0:T(8,128)(2,1)}) %reduce-scatter.2.cloned.1.call-update) | async-done | bytes 4112 | tf_op jit(solution)/shard_map/while/body/eval_jaxpr/reduce_scatter | solution.py:65
  281.7 0.7 convert_dynamic-update-slice_fusion.3
  282.5 0.7 divide_convert_fusion
  (56 shorter events, 2.0 us)
Async XLA Ops:
  6.5 67.4 %copy-start.1 = (bf16[64,8192]{1,0:T(8,128)(2,1)S(1)}, bf16[64,8192]{1,0:T(8,128)(2,1)}, u32[]{:S(2)}) copy-start(bf16[64,8192]{1,0:T(8,128)(2,1)} %param.7) | copy-start | bytes 3145732
  6.5 11.0 %copy-start = (bf16[64]{0:T(256)(128)(2,1)S(1)}, bf16[64]{0:T(256)(128)(2,1)}, u32[]{:S(2)}) copy-start(bf16[64]{0:T(256)(128)(2,1)} %param.8) | copy-start | bytes 388
  6.5 67.4 %collective-permute-start = (bf16[64,8192]{1,0:T(8,128)(2,1)}, bf16[64,8192]{1,0:T(8,128)(2,1)}, u32[]{:S(2)}, u32[]{:S(2)}) collective-permute-start(bf16[64,8192]{1,0:T(8,128)(2,1)} %param.7), channel_id=1, source_target_pairs={{0,30},{2,0},{4,2},{6,4},{8,6},{10,8},{12,10},{14,12},{16,14},{18,... | collective-permute-start | bytes 3145736 | tf_op jit(solution)/shard_map/ppermute | solution.py:11
  7.2 73.1 %collective-permute-start.5 = (bf16[64]{0:T(256)(128)(2,1)}, bf16[64]{0:T(256)(128)(2,1)S(1)}, u32[]{:S(2)}, u32[]{:S(2)}) collective-permute-start(bf16[64]{0:T(256)(128)(2,1)} %param.8), channel_id=1, source_target_pairs={{0,30},{2,0},{4,2},{6,4},{8,6},{10,8},{12,10},{14,12},{16,14},{18,... | collective-permute-start | bytes 392 | tf_op jit(solution)/shard_map/ppermute | solution.py:11
  75.4 38.3 %collective-permute-start.1 = (bf16[64,8192]{1,0:T(8,128)(2,1)S(1)}, bf16[64,8192]{1,0:T(8,128)(2,1)}, u32[]{:S(2)}, u32[]{:S(2)}) collective-permute-start(bf16[64,8192]{1,0:T(8,128)(2,1)S(1)} %get-tuple-element.128), channel_id=1, source_target_pairs={{0,28},{2,30},{4,0},{6,2},{8,4},{10,6},{12,8},{14,10},{16,12},{18,... | collective-permute-start | bytes 3145736 | tf_op jit(solution)/shard_map/ppermute | solution.py:11
  80.3 17.5 %collective-permute-start.6 = (bf16[64]{0:T(256)(128)(2,1)S(1)}, bf16[64]{0:T(256)(128)(2,1)S(1)}, u32[]{:S(2)}, u32[]{:S(2)}) collective-permute-start(bf16[64]{0:T(256)(128)(2,1)S(1)} %get-tuple-element.130), channel_id=1, source_target_pairs={{0,28},{2,30},{4,0},{6,2},{8,4},{10,6},{12,8},{14,10},{16,12},{18,... | collective-permute-start | bytes 392 | tf_op jit(solution)/shard_map/ppermute | solution.py:11
  85.1 26.1 %collective-permute-start.8 = (bf16[64]{0:T(256)(128)(2,1)S(1)}, bf16[64]{0:T(256)(128)(2,1)S(1)}, u32[]{:S(2)}, u32[]{:S(2)}) collective-permute-start(bf16[64]{0:T(256)(128)(2,1)S(1)} %get-tuple-element.131), channel_id=1, source_target_pairs={{0,28},{2,30},{4,0},{6,2},{8,4},{10,6},{12,8},{14,10},{16,12},{18,... | collective-permute-start | bytes 392 | tf_op jit(solution)/shard_map/ppermute | solution.py:11
  97.8 14.0 %collective-permute-start.7 = (bf16[64]{0:T(256)(128)(2,1)S(1)}, bf16[64]{0:T(256)(128)(2,1)S(1)}, u32[]{:S(2)}, u32[]{:S(2)}) collective-permute-start(bf16[64]{0:T(256)(128)(2,1)S(1)} %broadcast_select_fusion.8), channel_id=1, source_target_pairs={{0,24},{2,26},{4,28},{6,30},{8,0},{10,2},{12,4},{14,6},{16,8},{18,... | collective-permute-start | bytes 392 | tf_op jit(solution)/shard_map/ppermute | solution.py:11
  111.1 2.4 collective-permute-start.9
  113.6 23.1 %collective-permute-start.3 = (bf16[64,8192]{1,0:T(8,128)(2,1)S(1)}, bf16[64,8192]{1,0:T(8,128)(2,1)S(1)}, u32[]{:S(2)}, u32[]{:S(2)}) collective-permute-start(bf16[64,8192]{1,0:T(8,128)(2,1)S(1)} %get-tuple-element.129), channel_id=1, source_target_pairs={{0,28},{2,30},{4,0},{6,2},{8,4},{10,6},{12,8},{14,10},{16,12},{18,... | collective-permute-start | bytes 3145736 | tf_op jit(solution)/shard_map/ppermute | solution.py:11
  113.8 27.0 %collective-permute-start.2 = (bf16[64,8192]{1,0:T(8,128)(2,1)S(1)}, bf16[64,8192]{1,0:T(8,128)(2,1)S(1)}, u32[]{:S(2)}, u32[]{:S(2)}) collective-permute-start(bf16[64,8192]{1,0:T(8,128)(2,1)S(1)} %broadcast_select_fusion.3), channel_id=1, source_target_pairs={{0,24},{2,26},{4,28},{6,30},{8,0},{10,2},{12,4},{14,6},{16,8},{18,... | collective-permute-start | bytes 3145736 | tf_op jit(solution)/shard_map/ppermute | solution.py:11
  136.8 20.5 %collective-permute-start.4 = (bf16[64,8192]{1,0:T(8,128)(2,1)S(1)}, bf16[64,8192]{1,0:T(8,128)(2,1)S(1)}, u32[]{:S(2)}, u32[]{:S(2)}) collective-permute-start(bf16[64,8192]{1,0:T(8,128)(2,1)S(1)} %broadcast_select_fusion.1), channel_id=1, source_target_pairs={{0,24},{2,26},{4,28},{6,30},{8,0},{10,2},{12,4},{14,6},{16,8},{18,... | collective-permute-start | bytes 3145736 | tf_op jit(solution)/shard_map/ppermute | solution.py:11
  157.7 42.8 %reduce-scatter.2.cloned.1.call-start = ((), (), s32[]{:S(2)}) async-start(), calls=%async_computation.1 | async-start | bytes 24576 | tf_op jit(solution)/shard_map/while/body/eval_jaxpr/reduce_scatter | solution.py:65
  201.2 15.5 %reduce-scatter.2.cloned.1.call-start = ((), (), s32[]{:S(2)}) async-start(), calls=%async_computation.1 | async-start | bytes 24576 | tf_op jit(solution)/shard_map/while/body/eval_jaxpr/reduce_scatter | solution.py:65
  217.5 15.5 %reduce-scatter.2.cloned.1.call-start = ((), (), s32[]{:S(2)}) async-start(), calls=%async_computation.1 | async-start | bytes 24576 | tf_op jit(solution)/shard_map/while/body/eval_jaxpr/reduce_scatter | solution.py:65
  233.7 15.5 %reduce-scatter.2.cloned.1.call-start = ((), (), s32[]{:S(2)}) async-start(), calls=%async_computation.1 | async-start | bytes 24576 | tf_op jit(solution)/shard_map/while/body/eval_jaxpr/reduce_scatter | solution.py:65
  249.9 15.5 %reduce-scatter.2.cloned.1.call-start = ((), (), s32[]{:S(2)}) async-start(), calls=%async_computation.1 | async-start | bytes 24576 | tf_op jit(solution)/shard_map/while/body/eval_jaxpr/reduce_scatter | solution.py:65
  266.2 15.6 %reduce-scatter.2.cloned.1.call-start = ((), (), s32[]{:S(2)}) async-start(), calls=%async_computation.1 | async-start | bytes 24576 | tf_op jit(solution)/shard_map/while/body/eval_jaxpr/reduce_scatter | solution.py:65
Sparse Core Ops, SparseCore 0:
  163.5 36.9 reduce-scatter.1
  207.0 9.7 reduce-scatter.1
  223.2 9.7 reduce-scatter.1
  239.4 9.7 reduce-scatter.1
  255.7 9.7 reduce-scatter.1
  271.9 9.7 reduce-scatter.1
where the time goes:
time: 293 us; the launch traced here: 290 us
  waiting for transfers between devices  138 us (47%)
  blocking collectives  55.6 us (19%)
  starting transfers between devices  29.8 us (10%)
  loops' own time  23.6 us (8%)
  between operations  18.8 us (6%)
  local copies, waits for them, and re-layouts  9.45 us (3%)
  other arithmetic  8.33 us (3%)
  matrix products  6.33 us (2%)
    reduce_scatter x6, waiting for transfers between devices, step_each(): lax.psum_scatter(partial_value, 'fld', scatter_dimension=0, tiled=True)  85.8 us
    psum x1, blocking collectives, body(): lax.psum((jnp.where(owned[:, None], picked, 0.0), jnp.where(owned, picked...  55.6 us
    ppermute x10, waiting for transfers between devices, from_behind(): lax.ppermute(value, axis, [(i, (i + by) % peers) for i in range(peers)])  52.3 us
    ppermute x10, starting transfers between devices, from_behind(): lax.ppermute(value, axis, [(i, (i + by) % peers) for i in range(peers)])  29.8 us
    another operation x1, loops' own time, body(): lax.scan(step_each, jnp.zeros((), jnp.float32), step_ids)  23.6 us
    dot_general x6, matrix products, tile(): lax.dot_general(scaled, partner, (((1,), (1,)), ((), ())), preferred_elem...  6.33 us
  transfers between devices with their start and end apart: 16, of which 11 were waited for; matrix products, arithmetic and copies ran while one was open for 3% of the time, Pallas kernels for 0%

commit v1 on v0

v1 whole, which is shorter than its diff:
```python
import functools

import jax
import jax.numpy as jnp
from jax import lax
from jax.experimental import pallas as pl
from jax.experimental.pallas import tpu as pltpu
from jax.sharding import PartitionSpec as P

MESH = pl.DeviceIdType.MESH
LANES = 128


def kernel(
    dims, offsets, pivot_block, pivot_row, vectors, norms, out,
    gat, norm_src, norm_all, piv, acc, part, mate_in, total, recv,
    send1, recv1, own1, sendn, recvn, send2, recv2, send3, recv3,
):
    N, NF, G, C, subs, groups, rows, noff, npiv = dims
    share = rows // NF
    halves = NF // 2
    width = C // subs
    per = G // groups
    me, place = lax.axis_index("blk"), lax.axis_index("fld")
    group, chunk = me // G, me % G
    base = group * G
    core = me % 2
    mate = me + 1 - 2 * core
    slot = (chunk // 2) * NF + place

    barrier = pltpu.get_barrier_semaphore()

    def greet_blk(j, carry):
        pl.semaphore_signal(
            barrier, inc=1, device_id=(lax.rem(me + j, N), place), device_id_type=MESH
        )
        return carry

    def greet_fld(j, carry):
        other = lax.rem(place + 1 + j // G, NF)
        pl.semaphore_signal(
            barrier, inc=1, device_id=(base + j % G, other), device_id_type=MESH
        )
        return carry

    lax.fori_loop(1, N, greet_blk, 0)
    lax.fori_loop(0, G * (NF - 1), greet_fld, 0)

    norm_src[...] = jnp.zeros_like(norm_src)
    norm_src[0:1, 0:rows] = norms[...].astype(jnp.float32)
    norm_all[me] = norm_src[...]
    for sub in range(subs):
        pltpu.make_async_copy(
            vectors.at[:, pl.ds(pl.multiple_of(chunk * C + sub * width, LANES), width)],
            gat[sub].at[me], own1.at[sub],
        ).start()
    pl.semaphore_wait(barrier, (N - 1) + G * (NF - 1))

    def shift(k):
        d = (k + 1) // 2
        return N // 2 + d * (2 * (k % 2) - 1)

    def block_copy(sub, k):
        j = shift(k)
        peer = lax.rem(me + j, N)
        first = pl.multiple_of((peer % G) * C + sub * width, LANES)
        return pltpu.make_async_remote_copy(
            src_ref=vectors.at[:, pl.ds(first, width)], dst_ref=gat[sub].at[me],
            send_sem=send1.at[sub, j], recv_sem=recv1.at[sub, j],
            device_id=(peer, place), device_id_type=MESH,
        )

    def norm_copy(k):
        j = shift(k)
        peer = lax.rem(me + j, N)
        return pltpu.make_async_remote_copy(
            src_ref=norm_src, dst_ref=norm_all.at[me],
            send_sem=sendn.at[j], recv_sem=recvn.at[j],
            device_id=(peer, place), device_id_type=MESH,
        )

    def loop(count, step):
        def run(k, carry):
            step(k)
            return carry

        lax.fori_loop(0, count, run, 0)

    for sub in range(subs):
        loop(N - 1, lambda k, sub=sub: block_copy(sub, k).start())
    loop(N - 1, lambda k: norm_copy(k).start())

    def pivots(sub):
        spot = lax.broadcasted_iota(jnp.int32, (rows, width), 0)
        for t in range(noff):
            for s in range(npiv):
                block = gat[sub][pivot_block[t, s]].astype(jnp.float32)
                picked = jnp.sum(
                    jnp.where(spot == pivot_row[t, s], block, 0.0), axis=0, keepdims=True
                )
                piv[t * npiv + s] = jnp.broadcast_to(picked, (16, width)).astype(jnp.bfloat16)

    def tile(sub, i):
        block = base + i
        resident = gat[sub][block].reshape(rows // 16, 16, width)
        found = []
        for t in range(noff):
            partner = gat[sub][lax.rem(block + offsets[t], N)]
            scaled = jnp.concatenate(
                [
                    (resident * piv[t * npiv + s][None]).reshape(rows, width)
                    for s in range(npiv)
                ],
                axis=0,
            )
            found.append(
                lax.dot_general(
                    scaled, partner, (((1,), (1,)), ((), ())),
                    preferred_element_type=jnp.float32,
                )
            )
        value = jnp.concatenate(found, axis=1)
        for s in range(npiv):
            for h in range(NF):
                first = s * rows + h * share
                piece = value[first : first + share]
                if sub > 0:
                    piece = piece + acc[i, h % 2, h // 2, s]
                acc[i, h % 2, h // 2, s] = piece

    def mate_copy(q):
        return pltpu.make_async_remote_copy(
            src_ref=part.at[q], dst_ref=mate_in.at[q],
            send_sem=send2.at[q], recv_sem=recv2.at[q],
            device_id=(mate, place), device_id_type=MESH,
        )

    def total_copy(i, q):
        return pltpu.make_async_remote_copy(
            src_ref=total.at[i, q], dst_ref=recv.at[slot],
            send_sem=send3.at[i, q], recv_sem=recv3.at[slot],
            device_id=(base + i, 2 * q + core), device_id_type=MESH,
        )

    def is_self(i, q):
        return jnp.logical_and(base + i == me, 2 * q + core == place)

    def hand_out(g):
        mate_copy(g).wait_recv()

        def one(k):
            i = g * per + k
            total[i] = (acc[i, core] + mate_in[g, k].astype(jnp.float32)).astype(total.dtype)
            for q in range(halves):
                here = is_self(i, q)

                @pl.when(here)
                def _():
                    pltpu.make_async_copy(total.at[i, q], recv.at[slot], recv3.at[slot]).start()

                @pl.when(jnp.logical_not(here))
                def _():
                    total_copy(i, q).start()

        loop(per, one)

    for sub in range(subs):
        pltpu.make_async_copy(
            vectors.at[:, pl.ds(pl.multiple_of(chunk * C + sub * width, LANES), width)],
            gat[sub].at[me], own1.at[sub],
        ).wait()
        loop(N - 1, lambda k, sub=sub: block_copy(sub, k).wait_recv())
        pivots(sub)
        if sub < subs - 1:
            loop(G, lambda i, sub=sub: tile(sub, i))
    for g in range(groups):
        def one(k, g=g):
            i = g * per + k
            tile(subs - 1, i)
            part[g, k] = acc[i, 1 - core].astype(part.dtype)

        loop(per, one)
        mate_copy(g).start()
        if g > 0:
            hand_out(g - 1)
    hand_out(groups - 1)

    loop(N - 1, lambda k: norm_copy(k).wait_recv())
    lane = lax.broadcasted_iota(jnp.int32, (1, LANES), 1)
    line = lax.broadcasted_iota(jnp.int32, (share, LANES), 0)
    cols = lax.broadcasted_iota(jnp.int32, (share, LANES), 1)
    own_norms = jnp.sum(
        jnp.where(cols == line + place * share, norm_src[0:1, :], 0.0), axis=1, keepdims=True
    )
    partner_norms = [norm_all[lax.rem(me + offsets[t], N)][0:1, 0:rows] for t in range(noff)]
    divisors = []
    for t in range(noff):
        for s in range(npiv):
            row = norm_all[pivot_block[t, s]][0:1, :]
            pivot_norm = jnp.sum(
                jnp.where(lane == pivot_row[t, s], row, 0.0), axis=1, keepdims=True
            )
            divisors.append((own_norms * pivot_norm) * partner_norms[t])

    slots = (G // 2) * NF

    def arrived(k):
        pltpu.make_async_remote_copy(
            src_ref=total.at[0, 0], dst_ref=recv.at[k],
            send_sem=send3.at[0, 0], recv_sem=recv3.at[k],
            device_id=(mate, place), device_id_type=MESH,
        ).wait_recv()

    loop(slots, arrived)
    for s in range(npiv):
        whole = recv[0, s].astype(jnp.float32)
        for k in range(1, slots):
            whole = whole + recv[k, s].astype(jnp.float32)
        for t in range(noff):
            out[t, s] = (
                whole[:, t * rows : (t + 1) * rows] / divisors[t * npiv + s]
            ).astype(out.dtype)

    for sub in range(subs):
        loop(N - 1, lambda k, sub=sub: block_copy(sub, k).wait_send())
    loop(N - 1, lambda k: norm_copy(k).wait_send())
    for g in range(groups):
        mate_copy(g).wait_send()

    def sent(k):
        i, q = k // halves, k % halves

        @pl.when(jnp.logical_not(is_self(i, q)))
        def _():
            total_copy(i, q).wait_send()

    loop(G * halves, sent)


def body(vectors, norms, offsets, pivot_block, pivot_row):
    rows, fields = vectors.shape
    N, NF = lax.axis_size("blk"), lax.axis_size("fld")
    noff, npiv = pivot_block.shape
    G = min(N, fields // LANES)
    C = fields // G
    subs = 2 if C % (2 * LANES) == 0 else 1
    groups = 4
    share = rows // NF
    halves = NF // 2
    wire = jnp.bfloat16 if share % 16 == 0 else jnp.float32
    wide = noff * rows
    slots = (G // 2) * NF
    dims = (N, NF, G, C, subs, groups, rows, noff, npiv)
    dma = pltpu.SemaphoreType.DMA
    smem = pl.BlockSpec(memory_space=pltpu.SMEM)
    vmem = pl.BlockSpec(memory_space=pltpu.VMEM)
    return pl.pallas_call(
        functools.partial(kernel, dims),
        out_shape=jax.ShapeDtypeStruct((noff, npiv, share, rows), jnp.bfloat16),
        in_specs=[smem, smem, smem, pl.BlockSpec(memory_space=pl.ANY), vmem],
        out_specs=vmem,
        scratch_shapes=[
            tuple(pltpu.VMEM((N, rows, C // subs), jnp.bfloat16) for _ in range(subs)),
            pltpu.VMEM((8, LANES), jnp.float32),
            pltpu.VMEM((N, 8, LANES), jnp.float32),
            pltpu.VMEM((noff * npiv, 16, C // subs), jnp.bfloat16),
            pltpu.VMEM((G, 2, halves, npiv, share, wide), jnp.float32),
            pltpu.VMEM((groups, G // groups, halves, npiv, share, wide), wire),
            pltpu.VMEM((groups, G // groups, halves, npiv, share, wide), wire),
            pltpu.VMEM((G, halves, npiv, share, wide), wire),
            pltpu.VMEM((slots, npiv, share, wide), wire),
            dma((subs, N)),
            dma((subs, N)),
            dma((subs,)),
            dma((N,)),
            dma((N,)),
            dma((groups,)),
            dma((groups,)),
            dma((G, halves)),
            dma((slots,)),
        ],
        compiler_params=pltpu.CompilerParams(
            collective_id=0, has_side_effects=True, vmem_limit_bytes=32 * 1024 * 1024
        ),
        cost_estimate=pl.CostEstimate(
            flops=2 * noff * npiv * G * rows * rows * C,
            bytes_accessed=2 * rows * fields * 2,
            transcendentals=0,
        ),
    )(offsets, pivot_block, pivot_row, vectors, norms.reshape(1, rows))


def solution(mesh):
    return jax.shard_map(
        body,
        mesh=mesh,
        in_specs=(P("blk", "fld"), P("blk"), P(), P(), P()),
        out_specs=P(None, None, ("blk", "fld"), None),
        check_vma=False,
    )
```

time: 293 us -> 50.4 us (0.17)
  the two profiles are of different devices: /device:TPU:5 before, /device:TPU:29 now
where the time goes in v1:
time: 50.4 us; the launch traced here: 50.2 us
  Pallas kernels  46.3 us (92%)
  local copies, waits for them, and re-layouts  3.86 us (8%)
    pallas_call x1, Pallas kernels, body(): pl.pallas_call(functools.partial(kernel, dims), out_shape=jax.ShapeDtypeS...  46.3 us
    unnamed x11, local copies, waits for them, and re-layouts  3.86 us

profile of v1, /device:TPU:29, one launch (start us, length us, event | category | flops | bytes accessed | tf_op | source)
XLA Modules:
  0.0 50.2 jit_solution(7244741240773373002)
XLA Ops:
  0.0 0.0 copy-start.1
  0.0 0.0 copy-start.3
  0.0 0.7 %copy-done.1 = s32[2,3]{1,0:T(2,128)S(1)} copy-done((s32[2,3]{1,0:T(2,128)S(1)}, s32[2,3]{1,0:T(2,128)}, u32[]{:S(2)}) %copy-start.1) | copy-done | bytes 48
  0.7 0.0 copy-done.3
  0.7 0.0 copy-start
  0.7 1.2 %copy-done = bf16[64,8192]{1,0:T(8,128)(2,1)S(1)} copy-done((bf16[64,8192]{1,0:T(8,128)(2,1)S(1)}, bf16[64,8192]{1,0:T(8,128)(2,1)}, u32[]{:S(2)}) %copy-start) | copy-done | bytes 1048600
  1.9 0.0 copy-start.2
  1.9 0.7 %copy-done.2 = s32[2,3]{1,0:T(2,128)S(1)} copy-done((s32[2,3]{1,0:T(2,128)S(1)}, s32[2,3]{1,0:T(2,128)}, u32[]{:S(2)}) %copy-start.2) | copy-done | bytes 48
  2.6 0.0 copy-start.4
  2.6 0.7 %copy-done.4 = bf16[64]{0:T(256)(128)(2,1)S(1)} copy-done((bf16[64]{0:T(256)(128)(2,1)S(1)}, bf16[64]{0:T(256)(128)(2,1)}, u32[]{:S(2)}) %copy-start.4) | copy-done | bytes 152
  3.2 46.3 %shard_map.55 = bf16[2,3,32,64]{3,2,1,0:T(8,128)(2,1)S(1)} custom-call(s32[2]{0:T(128)S(1)} %copy-done.3, s32[2,3]{1,0:T(2,128)S(1)} %copy-done.1, s32[2,3]{1,0:T(2,128)S(1)} %copy-done.2, bf16[64,8192]{1,0:T(8,128)(2,1)S(1)} %copy-done, bf16[1,64]{1,0:T(2,128)(2,1)S(1)} %bitcast.1), custom_call_target="tpu_custom_call" | custom-call | flops 402653184 | bytes 2097152 | tf_op jit(solution)/shard_map/pallas_call | solution.py:257
  49.5 0.6 %copy.7 = bf16[2,3,32,64]{3,2,1,0:T(8,128)(2,1)} copy(bf16[2,3,32,64]{3,2,1,0:T(8,128)(2,1)S(1)} %shard_map.55) | data formatting | bytes 49152
Async XLA Ops:
  0.0 0.7 %copy-start.1 = (s32[2,3]{1,0:T(2,128)S(1)}, s32[2,3]{1,0:T(2,128)}, u32[]{:S(2)}) copy-start(s32[2,3]{1,0:T(2,128)} %pivot_block.1) | copy-start | bytes 76
  0.0 0.7 %copy-start.3 = (s32[2]{0:T(128)S(1)}, s32[2]{0:T(128)}, u32[]{:S(2)}) copy-start(s32[2]{0:T(128)} %offsets.1) | copy-start | bytes 28
  0.7 1.2 %copy-start = (bf16[64,8192]{1,0:T(8,128)(2,1)S(1)}, bf16[64,8192]{1,0:T(8,128)(2,1)}, u32[]{:S(2)}) copy-start(bf16[64,8192]{1,0:T(8,128)(2,1)} %vectors.1) | copy-start | bytes 3145732
  1.9 0.7 %copy-start.2 = (s32[2,3]{1,0:T(2,128)S(1)}, s32[2,3]{1,0:T(2,128)}, u32[]{:S(2)}) copy-start(s32[2,3]{1,0:T(2,128)} %pivot_row.1) | copy-start | bytes 76
  2.6 0.7 %copy-start.4 = (bf16[64]{0:T(256)(128)(2,1)S(1)}, bf16[64]{0:T(256)(128)(2,1)}, u32[]{:S(2)}) copy-start(bf16[64]{0:T(256)(128)(2,1)} %param.6) | copy-start | bytes 388

commit v2 on v1

--- a/solution.py
+++ b/solution.py
@@ -12,14 +12,15 @@
 
 
 def kernel(
-    dims, offsets, pivot_block, pivot_row, vectors, norms, out,
-    gat, norm_src, norm_all, piv, acc, part, mate_in, total, recv,
+    dims, offsets_in, pivot_block_in, pivot_row_in, vectors, norms_in, out,
+    offsets, pivot_block, pivot_row, norms, small, gat, norm_src, norm_all, piv, acc, part, mate_in, total, recv,
     send1, recv1, own1, sendn, recvn, send2, recv2, send3, recv3,
 ):
-    N, NF, G, C, subs, groups, rows, noff, npiv = dims
+    N, NF, G, C, widths, groups, rows, noff, npiv = dims
     share = rows // NF
     halves = NF // 2
-    width = C // subs
+    subs = len(widths)
+    starts = [sum(widths[:sub]) for sub in range(subs)]
     per = G // groups
     me, place = lax.axis_index("blk"), lax.axis_index("fld")
     group, chunk = me // G, me % G
@@ -46,14 +47,28 @@
     lax.fori_loop(1, N, greet_blk, 0)
     lax.fori_loop(0, G * (NF - 1), greet_fld, 0)
 
+    smalls = [
+        pltpu.make_async_copy(src, dst, small.at[k])
+        for k, (src, dst) in enumerate((
+            (norms_in, norms), (offsets_in, offsets),
+            (pivot_block_in, pivot_block), (pivot_row_in, pivot_row),
+        ))
+    ]
+
+    def own_copy(sub):
+        first = pl.multiple_of(chunk * C + starts[sub], LANES)
+        return pltpu.make_async_copy(
+            vectors.at[:, pl.ds(first, widths[sub])], gat[sub].at[me], own1.at[sub]
+        )
+
+    for copy in smalls:
+        copy.start()
+    for sub in range(subs):
+        own_copy(sub).start()
     norm_src[...] = jnp.zeros_like(norm_src)
+    smalls[0].wait()
     norm_src[0:1, 0:rows] = norms[...].astype(jnp.float32)
     norm_all[me] = norm_src[...]
-    for sub in range(subs):
-        pltpu.make_async_copy(
-            vectors.at[:, pl.ds(pl.multiple_of(chunk * C + sub * width, LANES), width)],
-            gat[sub].at[me], own1.at[sub],
-        ).start()
     pl.semaphore_wait(barrier, (N - 1) + G * (NF - 1))
 
     def shift(k):
@@ -63,9 +78,9 @@
     def block_copy(sub, k):
         j = shift(k)
         peer = lax.rem(me + j, N)
-        first = pl.multiple_of((peer % G) * C + sub * width, LANES)
+        first = pl.multiple_of((peer % G) * C + starts[sub], LANES)
         return pltpu.make_async_remote_copy(
-            src_ref=vectors.at[:, pl.ds(first, width)], dst_ref=gat[sub].at[me],
+            src_ref=vectors.at[:, pl.ds(first, widths[sub])], dst_ref=gat[sub].at[me],
             send_sem=send1.at[sub, j], recv_sem=recv1.at[sub, j],
             device_id=(peer, place), device_id_type=MESH,
         )
@@ -90,7 +105,11 @@
         loop(N - 1, lambda k, sub=sub: block_copy(sub, k).start())
     loop(N - 1, lambda k: norm_copy(k).start())
 
+    for copy in smalls[1:]:
+        copy.wait()
+
     def pivots(sub):
+        width = widths[sub]
         spot = lax.broadcasted_iota(jnp.int32, (rows, width), 0)
         for t in range(noff):
             for s in range(npiv):
@@ -98,17 +117,17 @@
                 picked = jnp.sum(
                     jnp.where(spot == pivot_row[t, s], block, 0.0), axis=0, keepdims=True
                 )
-                piv[t * npiv + s] = jnp.broadcast_to(picked, (16, width)).astype(jnp.bfloat16)
+                piv[t * npiv + s, :, 0:width] = jnp.broadcast_to(picked, (16, width)).astype(jnp.bfloat16)
 
     def tile(sub, i):
-        block = base + i
+        block, width = base + i, widths[sub]
         resident = gat[sub][block].reshape(rows // 16, 16, width)
         found = []
         for t in range(noff):
             partner = gat[sub][lax.rem(block + offsets[t], N)]
             scaled = jnp.concatenate(
                 [
-                    (resident * piv[t * npiv + s][None]).reshape(rows, width)
+                    (resident * piv[t * npiv + s, :, 0:width][None]).reshape(rows, width)
                     for s in range(npiv)
                 ],
                 axis=0,
@@ -165,21 +184,20 @@
         loop(per, one)
 
     for sub in range(subs):
-        pltpu.make_async_copy(
-            vectors.at[:, pl.ds(pl.multiple_of(chunk * C + sub * width, LANES), width)],
-            gat[sub].at[me], own1.at[sub],
-        ).wait()
+        own_copy(sub).wait()
         loop(N - 1, lambda k, sub=sub: block_copy(sub, k).wait_recv())
         pivots(sub)
         if sub < subs - 1:
-            loop(G, lambda i, sub=sub: tile(sub, i))
+            def several(g, sub=sub):
+                for k in range(per):
+                    tile(sub, g * per + k)
+
+            loop(groups, several)
     for g in range(groups):
-        def one(k, g=g):
-            i = g * per + k
-            tile(subs - 1, i)
-            part[g, k] = acc[i, 1 - core].astype(part.dtype)
-
-        loop(per, one)
+        for k in range(per):
+            tile(subs - 1, g * per + k)
+        for k in range(per):
+            part[g, k] = acc[g * per + k, 1 - core].astype(part.dtype)
         mate_copy(g).start()
         if g > 0:
             hand_out(g - 1)
@@ -243,27 +261,32 @@
     noff, npiv = pivot_block.shape
     G = min(N, fields // LANES)
     C = fields // G
-    subs = 2 if C % (2 * LANES) == 0 else 1
+    widths = (C - LANES, LANES) if C > LANES else (C,)
     groups = 4
     share = rows // NF
     halves = NF // 2
     wire = jnp.bfloat16 if share % 16 == 0 else jnp.float32
     wide = noff * rows
     slots = (G // 2) * NF
-    dims = (N, NF, G, C, subs, groups, rows, noff, npiv)
+    subs = len(widths)
+    dims = (N, NF, G, C, widths, groups, rows, noff, npiv)
     dma = pltpu.SemaphoreType.DMA
-    smem = pl.BlockSpec(memory_space=pltpu.SMEM)
-    vmem = pl.BlockSpec(memory_space=pltpu.VMEM)
+    anywhere = pl.BlockSpec(memory_space=pl.ANY)
     return pl.pallas_call(
         functools.partial(kernel, dims),
         out_shape=jax.ShapeDtypeStruct((noff, npiv, share, rows), jnp.bfloat16),
-        in_specs=[smem, smem, smem, pl.BlockSpec(memory_space=pl.ANY), vmem],
-        out_specs=vmem,
+        in_specs=[anywhere] * 5,
+        out_specs=pl.BlockSpec(memory_space=pltpu.VMEM),
         scratch_shapes=[
-            tuple(pltpu.VMEM((N, rows, C // subs), jnp.bfloat16) for _ in range(subs)),
+            pltpu.SMEM(offsets.shape, jnp.int32),
+            pltpu.SMEM(pivot_block.shape, jnp.int32),
+            pltpu.SMEM(pivot_row.shape, jnp.int32),
+            pltpu.VMEM((1, rows), jnp.bfloat16),
+            dma((4,)),
+            tuple(pltpu.VMEM((N, rows, width), jnp.bfloat16) for width in widths),
             pltpu.VMEM((8, LANES), jnp.float32),
             pltpu.VMEM((N, 8, LANES), jnp.float32),
-            pltpu.VMEM((noff * npiv, 16, C // subs), jnp.bfloat16),
+            pltpu.VMEM((noff * npiv, 16, max(widths)), jnp.bfloat16),
             pltpu.VMEM((G, 2, halves, npiv, share, wide), jnp.float32),
             pltpu.VMEM((groups, G // groups, halves, npiv, share, wide), wire),
             pltpu.VMEM((groups, G // groups, halves, npiv, share, wide), wire),
@@ -280,7 +303,7 @@
             dma((slots,)),
         ],
         compiler_params=pltpu.CompilerParams(
-            collective_id=0, has_side_effects=True, vmem_limit_bytes=32 * 1024 * 1024
+            collective_id=0, has_side_effects=True, vmem_limit_bytes=63 * 1024 * 1024
         ),
         cost_estimate=pl.CostEstimate(
             flops=2 * noff * npiv * G * rows * rows * C,

time: 50.4 us -> 47 us (0.933)
  the two profiles are of different devices: /device:TPU:29 before, /device:TPU:25 now
where the time goes in v2:
time: 47 us; the launch traced here: 46.8 us
  Pallas kernels  45.3 us (96%)
  local copies, waits for them, and re-layouts  1.42 us (3%)
    pallas_call x1, Pallas kernels, body(): pl.pallas_call(functools.partial(kernel, dims), out_shape=jax.ShapeDtypeS...  45.3 us
    unnamed x1, local copies, waits for them, and re-layouts  1.42 us

profile of v2, /device:TPU:25, one launch (start us, length us, event | category | flops | bytes accessed | tf_op | source)
XLA Modules:
  0.0 46.8 jit_solution(13825536181738626251)
XLA Ops:
  0.0 45.3 %shard_map.55 = bf16[2,3,32,64]{3,2,1,0:T(8,128)(2,1)} custom-call(s32[2]{0:T(128)} %offsets_in.1, s32[2,3]{1,0:T(2,128)} %pivot_block_in.1, s32[2,3]{1,0:T(2,128)} %pivot_row_in.1, bf16[64,8192]{1,0:T(8,128)(2,1)} %vectors.1, bf16[1,64]{1,0:T(2,128)(2,1)} %bitcast.1), custom_call_target="tpu_custom_call" | custom-call | flops 402653184 | bytes 2097152 | tf_op jit(solution)/shard_map/pallas_call | solution.py:275
  45.3 1.4 %copy.7 = bf16[2,3,32,64]{3,2,1,0:T(8,128)(2,1)} copy(bf16[2,3,32,64]{3,2,1,0:T(8,128)(2,1)} %shard_map.55) | data formatting | bytes 49152

commit v3 on v2

--- a/solution.py
+++ b/solution.py
@@ -71,27 +71,28 @@
     norm_all[me] = norm_src[...]
     pl.semaphore_wait(barrier, (N - 1) + G * (NF - 1))
 
-    def shift(k):
-        d = (k + 1) // 2
-        return N // 2 + d * (2 * (k % 2) - 1)
+    side = N // 2
+
+    def peer_of(k):
+        half, spot = me // side, me % side
+        other = k % 2 == 0
+        turn = lax.rem(spot + (k + 1) // 2, side)
+        return jnp.where(other, 1 - half, half) * side + turn
 
     def block_copy(sub, k):
-        j = shift(k)
-        peer = lax.rem(me + j, N)
+        peer = peer_of(k)
         first = pl.multiple_of((peer % G) * C + starts[sub], LANES)
         return pltpu.make_async_remote_copy(
             src_ref=vectors.at[:, pl.ds(first, widths[sub])], dst_ref=gat[sub].at[me],
-            send_sem=send1.at[sub, j], recv_sem=recv1.at[sub, j],
+            send_sem=send1.at[sub, k], recv_sem=recv1.at[sub, k],
             device_id=(peer, place), device_id_type=MESH,
         )
 
     def norm_copy(k):
-        j = shift(k)
-        peer = lax.rem(me + j, N)
         return pltpu.make_async_remote_copy(
             src_ref=norm_src, dst_ref=norm_all.at[me],
-            send_sem=sendn.at[j], recv_sem=recvn.at[j],
-            device_id=(peer, place), device_id_type=MESH,
+            send_sem=sendn.at[k], recv_sem=recvn.at[k],
+            device_id=(peer_of(k), place), device_id_type=MESH,
         )
 
     def loop(count, step):

time: 47 us -> 46.7 us (level)
  no operation moved by 1% of the time
where the time goes in v3:
time: 46.7 us; the launch traced here: 46.5 us
  Pallas kernels  45 us (96%)
  local copies, waits for them, and re-layouts  1.42 us (3%)
    pallas_call x1, Pallas kernels, body(): pl.pallas_call(functools.partial(kernel, dims), out_shape=jax.ShapeDtypeS...  45 us
    unnamed x1, local copies, waits for them, and re-layouts  1.42 us

profile of v3, /device:TPU:25, one launch (start us, length us, event | category | flops | bytes accessed | tf_op | source)
XLA Modules:
  0.0 46.5 jit_solution(6378357510312091176)
XLA Ops:
  0.0 45.0 %shard_map.55 = bf16[2,3,32,64]{3,2,1,0:T(8,128)(2,1)} custom-call(s32[2]{0:T(128)} %offsets_in.1, s32[2,3]{1,0:T(2,128)} %pivot_block_in.1, s32[2,3]{1,0:T(2,128)} %pivot_row_in.1, bf16[64,8192]{1,0:T(8,128)(2,1)} %vectors.1, bf16[1,64]{1,0:T(2,128)(2,1)} %bitcast.1), custom_call_target="tpu_custom_call" | custom-call | flops 402653184 | bytes 2097152 | tf_op jit(solution)/shard_map/pallas_call | solution.py:276
  45.0 1.4 %copy.7 = bf16[2,3,32,64]{3,2,1,0:T(8,128)(2,1)} copy(bf16[2,3,32,64]{3,2,1,0:T(8,128)(2,1)} %shard_map.55) | data formatting | bytes 49152

commit v4 on v3

--- a/solution.py
+++ b/solution.py
@@ -13,8 +13,8 @@
 
 def kernel(
     dims, offsets_in, pivot_block_in, pivot_row_in, vectors, norms_in, out,
-    offsets, pivot_block, pivot_row, norms, small, gat, norm_src, norm_all, piv, acc, part, mate_in, total, recv,
-    send1, recv1, own1, sendn, recvn, send2, recv2, send3, recv3,
+    offsets, pivot_block, pivot_row, norms, small, gat, norm_src, norm_all, piv, acc, part, mate_in, total, cross_in, final, recv,
+    send1, recv1, own1, sendn, recvn, send2, recv2, sendx, recvx, send3, recv3,
 ):
     N, NF, G, C, widths, groups, rows, noff, npiv = dims
     share = rows // NF
@@ -27,7 +27,8 @@
     base = group * G
     core = me % 2
     mate = me + 1 - 2 * core
-    slot = (chunk // 2) * NF + place
+    slot = chunk // 2
+    gathers = place % 2 == core
 
     barrier = pltpu.get_barrier_semaphore()
 
@@ -38,14 +39,13 @@
         return carry
 
     def greet_fld(j, carry):
-        other = lax.rem(place + 1 + j // G, NF)
         pl.semaphore_signal(
-            barrier, inc=1, device_id=(base + j % G, other), device_id_type=MESH
+            barrier, inc=1, device_id=(me, lax.rem(place + j, NF)), device_id_type=MESH
         )
         return carry
 
     lax.fori_loop(1, N, greet_blk, 0)
-    lax.fori_loop(0, G * (NF - 1), greet_fld, 0)
+    lax.fori_loop(1, NF, greet_fld, 0)
 
     smalls = [
         pltpu.make_async_copy(src, dst, small.at[k])
@@ -69,7 +69,7 @@
     smalls[0].wait()
     norm_src[0:1, 0:rows] = norms[...].astype(jnp.float32)
     norm_all[me] = norm_src[...]
-    pl.semaphore_wait(barrier, (N - 1) + G * (NF - 1))
+    pl.semaphore_wait(barrier, (N - 1) + (NF - 1))
 
     side = N // 2
 
@@ -120,8 +120,11 @@
                 )
                 piv[t * npiv + s, :, 0:width] = jnp.broadcast_to(picked, (16, width)).astype(jnp.bfloat16)
 
-    def tile(sub, i):
-        block, width = base + i, widths[sub]
+    def index(g, k):
+        return k * groups + (g + (groups // 2) * (k % 2)) % groups
+
+    def tile(sub, g, k):
+        block, width = base + index(g, k), widths[sub]
         resident = gat[sub][block].reshape(rows // 16, 16, width)
         found = []
         for t in range(noff):
@@ -145,8 +148,8 @@
                 first = s * rows + h * share
                 piece = value[first : first + share]
                 if sub > 0:
-                    piece = piece + acc[i, h % 2, h // 2, s]
-                acc[i, h % 2, h // 2, s] = piece
+                    piece = piece + acc[g, k, h % 2, h // 2, s]
+                acc[g, k, h % 2, h // 2, s] = piece
 
     def mate_copy(q):
         return pltpu.make_async_remote_copy(
@@ -155,34 +158,59 @@
             device_id=(mate, place), device_id_type=MESH,
         )
 
-    def total_copy(i, q):
-        return pltpu.make_async_remote_copy(
-            src_ref=total.at[i, q], dst_ref=recv.at[slot],
-            send_sem=send3.at[i, q], recv_sem=recv3.at[slot],
-            device_id=(base + i, 2 * q + core), device_id_type=MESH,
-        )
-
-    def is_self(i, q):
-        return jnp.logical_and(base + i == me, 2 * q + core == place)
-
-    def hand_out(g):
+    def cross_copy(g, q):
+        target = 2 * q + core
+        lane = lax.rem(place - target + NF, NF) - 1
+        return pltpu.make_async_remote_copy(
+            src_ref=total.at[g, q], dst_ref=cross_in.at[g, lane],
+            send_sem=sendx.at[g, q], recv_sem=recvx.at[g, lane],
+            device_id=(me, target), device_id_type=MESH,
+        )
+
+    def cross_arrival(g, lane):
+        return pltpu.make_async_remote_copy(
+            src_ref=total.at[g, 0], dst_ref=cross_in.at[g, lane],
+            send_sem=sendx.at[g, 0], recv_sem=recvx.at[g, lane],
+            device_id=(me, lax.rem(place + 1, NF)), device_id_type=MESH,
+        )
+
+    def final_copy(g, k):
+        return pltpu.make_async_remote_copy(
+            src_ref=final.at[g, k], dst_ref=recv.at[slot],
+            send_sem=send3.at[g, k], recv_sem=recv3.at[slot],
+            device_id=(base + index(g, k), place), device_id_type=MESH,
+        )
+
+    def over_fld(g):
         mate_copy(g).wait_recv()
-
-        def one(k):
-            i = g * per + k
-            total[i] = (acc[i, core] + mate_in[g, k].astype(jnp.float32)).astype(total.dtype)
-            for q in range(halves):
-                here = is_self(i, q)
+        for q in range(halves):
+            @pl.when(2 * q + core != place)
+            def _():
+                for k in range(per):
+                    total[g, q, k] = (
+                        acc[g, k, core, q] + mate_in[g, k, q].astype(jnp.float32)
+                    ).astype(total.dtype)
+                cross_copy(g, q).start()
+
+    def over_blk(g):
+        @pl.when(gathers)
+        def _():
+            for lane in range(NF - 1):
+                cross_arrival(g, lane).wait_recv()
+            for k in range(per):
+                whole = acc[g, k, core, place // 2] + mate_in[g, k, place // 2].astype(jnp.float32)
+                for lane in range(NF - 1):
+                    whole = whole + cross_in[g, lane, k].astype(jnp.float32)
+                final[g, k] = whole.astype(final.dtype)
+                here = base + index(g, k) == me
 
                 @pl.when(here)
                 def _():
-                    pltpu.make_async_copy(total.at[i, q], recv.at[slot], recv3.at[slot]).start()
+                    pltpu.make_async_copy(final.at[g, k], recv.at[slot], recv3.at[slot]).start()
 
                 @pl.when(jnp.logical_not(here))
                 def _():
-                    total_copy(i, q).start()
-
-        loop(per, one)
+                    final_copy(g, k).start()
 
     for sub in range(subs):
         own_copy(sub).wait()
@@ -191,18 +219,23 @@
         if sub < subs - 1:
             def several(g, sub=sub):
                 for k in range(per):
-                    tile(sub, g * per + k)
+                    tile(sub, g, k)
 
             loop(groups, several)
     for g in range(groups):
         for k in range(per):
-            tile(subs - 1, g * per + k)
+            tile(subs - 1, g, k)
         for k in range(per):
-            part[g, k] = acc[g * per + k, 1 - core].astype(part.dtype)
+            part[g, k] = acc[g, k, 1 - core].astype(part.dtype)
         mate_copy(g).start()
         if g > 0:
-            hand_out(g - 1)
-    hand_out(groups - 1)
+            over_fld(g - 1)
+        if g > 1:
+            over_blk(g - 2)
+    over_fld(groups - 1)
+    if groups > 1:
+        over_blk(groups - 2)
+    over_blk(groups - 1)
 
     loop(N - 1, lambda k: norm_copy(k).wait_recv())
     lane = lax.broadcasted_iota(jnp.int32, (1, LANES), 1)
@@ -221,11 +254,11 @@
             )
             divisors.append((own_norms * pivot_norm) * partner_norms[t])
 
-    slots = (G // 2) * NF
+    slots = G // 2
 
     def arrived(k):
         pltpu.make_async_remote_copy(
-            src_ref=total.at[0, 0], dst_ref=recv.at[k],
+            src_ref=final.at[0, 0], dst_ref=recv.at[k],
             send_sem=send3.at[0, 0], recv_sem=recv3.at[k],
             device_id=(mate, place), device_id_type=MESH,
         ).wait_recv()
@@ -246,14 +279,22 @@
     for g in range(groups):
         mate_copy(g).wait_send()
 
-    def sent(k):
-        i, q = k // halves, k % halves
-
-        @pl.when(jnp.logical_not(is_self(i, q)))
+    for g in range(groups):
+        for q in range(halves):
+            @pl.when(2 * q + core != place)
+            def _():
+                cross_copy(g, q).wait_send()
+
+    def sent(j):
+        g, k = j // per, j % per
+
+        @pl.when(base + index(g, k) != me)
         def _():
-            total_copy(i, q).wait_send()
-
-    loop(G * halves, sent)
+            final_copy(g, k).wait_send()
+
+    @pl.when(gathers)
+    def _():
+        loop(G, sent)
 
 
 def body(vectors, norms, offsets, pivot_block, pivot_row):
@@ -263,12 +304,13 @@
     G = min(N, fields // LANES)
     C = fields // G
     widths = (C - LANES, LANES) if C > LANES else (C,)
-    groups = 4
+    groups = 4 if G % 4 == 0 else 1
+    per = G // groups
     share = rows // NF
     halves = NF // 2
     wire = jnp.bfloat16 if share % 16 == 0 else jnp.float32
     wide = noff * rows
-    slots = (G // 2) * NF
+    slots = G // 2
     subs = len(widths)
     dims = (N, NF, G, C, widths, groups, rows, noff, npiv)
     dma = pltpu.SemaphoreType.DMA
@@ -288,10 +330,12 @@
             pltpu.VMEM((8, LANES), jnp.float32),
             pltpu.VMEM((N, 8, LANES), jnp.float32),
             pltpu.VMEM((noff * npiv, 16, max(widths)), jnp.bfloat16),
-            pltpu.VMEM((G, 2, halves, npiv, share, wide), jnp.float32),
-            pltpu.VMEM((groups, G // groups, halves, npiv, share, wide), wire),
-            pltpu.VMEM((groups, G // groups, halves, npiv, share, wide), wire),
-            pltpu.VMEM((G, halves, npiv, share, wide), wire),
+            pltpu.VMEM((groups, per, 2, halves, npiv, share, wide), jnp.float32),
+            pltpu.VMEM((groups, per, halves, npiv, share, wide), wire),
+            pltpu.VMEM((groups, per, halves, npiv, share, wide), wire),
+            pltpu.VMEM((groups, halves, per, npiv, share, wide), wire),
+            pltpu.VMEM((groups, NF - 1, per, npiv, share, wide), wire),
+            pltpu.VMEM((groups, per, npiv, share, wide), wire),
             pltpu.VMEM((slots, npiv, share, wide), wire),
             dma((subs, N)),
             dma((subs, N)),
@@ -300,7 +344,9 @@
             dma((N,)),
             dma((groups,)),
             dma((groups,)),
-            dma((G, halves)),
+            dma((groups, halves)),
+            dma((groups, NF - 1)),
+            dma((groups, per)),
             dma((slots,)),
         ],
         compiler_params=pltpu.CompilerParams(

time: 46.7 us -> 47 us (level)
  the two profiles are of different devices: /device:TPU:25 before, /device:TPU:5 now
where the time goes in v4:
time: 47 us; the launch traced here: 46.8 us
  Pallas kernels  45.3 us (96%)
  local copies, waits for them, and re-layouts  1.42 us (3%)
    pallas_call x1, Pallas kernels, body(): pl.pallas_call(functools.partial(kernel, dims), out_shape=jax.ShapeDtypeS...  45.3 us
    unnamed x1, local copies, waits for them, and re-layouts  1.42 us

profile of v4, /device:TPU:5, one launch (start us, length us, event | category | flops | bytes accessed | tf_op | source)
XLA Modules:
  0.0 46.8 jit_solution(2810318166072064630)
XLA Ops:
  0.0 45.3 %shard_map.55 = bf16[2,3,32,64]{3,2,1,0:T(8,128)(2,1)} custom-call(s32[2]{0:T(128)} %offsets_in.1, s32[2,3]{1,0:T(2,128)} %pivot_block_in.1, s32[2,3]{1,0:T(2,128)} %pivot_row_in.1, bf16[64,8192]{1,0:T(8,128)(2,1)} %vectors.1, bf16[1,64]{1,0:T(2,128)(2,1)} %bitcast.1), custom_call_target="tpu_custom_call" | custom-call | flops 402653184 | bytes 2097152 | tf_op jit(solution)/shard_map/pallas_call | solution.py:318
  45.3 1.4 %copy.7 = bf16[2,3,32,64]{3,2,1,0:T(8,128)(2,1)} copy(bf16[2,3,32,64]{3,2,1,0:T(8,128)(2,1)} %shard_map.55) | data formatting | bytes 49152

commit v5 on v4

--- a/solution.py
+++ b/solution.py
@@ -126,23 +126,26 @@
     def tile(sub, g, k):
         block, width = base + index(g, k), widths[sub]
         resident = gat[sub][block].reshape(rows // 16, 16, width)
-        found = []
-        for t in range(noff):
-            partner = gat[sub][lax.rem(block + offsets[t], N)]
-            scaled = jnp.concatenate(
-                [
-                    (resident * piv[t * npiv + s, :, 0:width][None]).reshape(rows, width)
-                    for s in range(npiv)
-                ],
-                axis=0,
+        ahead = [block + offsets[t] for t in range(noff)]
+        partner = jnp.concatenate(
+            [gat[sub][jnp.where(b < N, b, b - N)] for b in ahead], axis=0
+        )
+        scaled = jnp.concatenate(
+            [
+                (resident * piv[j, :, 0:width][None]).reshape(rows, width)
+                for j in range(noff * npiv)
+            ],
+            axis=0,
+        )
+        met = lax.dot_general(
+            scaled, partner, (((1,), (1,)), ((), ())), preferred_element_type=jnp.float32
+        )
+        lane = lax.broadcasted_iota(jnp.int32, (npiv * rows, noff * rows), 1)
+        value = met[0 : npiv * rows]
+        for t in range(1, noff):
+            value = jnp.where(
+                lane < t * rows, value, met[t * npiv * rows : (t + 1) * npiv * rows]
             )
-            found.append(
-                lax.dot_general(
-                    scaled, partner, (((1,), (1,)), ((), ())),
-                    preferred_element_type=jnp.float32,
-                )
-            )
-        value = jnp.concatenate(found, axis=1)
         for s in range(npiv):
             for h in range(NF):
                 first = s * rows + h * share
@@ -303,7 +306,8 @@
     noff, npiv = pivot_block.shape
     G = min(N, fields // LANES)
     C = fields // G
-    widths = (C - LANES, LANES) if C > LANES else (C,)
+    tail = min(2, C // LANES - 1)
+    widths = (C - tail * LANES,) + (LANES,) * tail
     groups = 4 if G % 4 == 0 else 1
     per = G // groups
     share = rows // NF

time: 47 us -> 47.3 us (level)
  no operation moved by 1% of the time
where the time goes in v5:
time: 47.3 us; the launch traced here: 47.1 us
  Pallas kernels  45.7 us (97%)
  local copies, waits for them, and re-layouts  1.42 us (3%)
    pallas_call x1, Pallas kernels, body(): pl.pallas_call(functools.partial(kernel, dims), out_shape=jax.ShapeDtypeS...  45.7 us
    unnamed x1, local copies, waits for them, and re-layouts  1.42 us

profile of v5, /device:TPU:5, one launch (start us, length us, event | category | flops | bytes accessed | tf_op | source)
XLA Modules:
  0.0 47.1 jit_solution(18401484104753914364)
XLA Ops:
  0.0 45.7 %shard_map.55 = bf16[2,3,32,64]{3,2,1,0:T(8,128)(2,1)} custom-call(s32[2]{0:T(128)} %offsets_in.1, s32[2,3]{1,0:T(2,128)} %pivot_block_in.1, s32[2,3]{1,0:T(2,128)} %pivot_row_in.1, bf16[64,8192]{1,0:T(8,128)(2,1)} %vectors.1, bf16[1,64]{1,0:T(2,128)(2,1)} %bitcast.1), custom_call_target="tpu_custom_call" | custom-call | flops 402653184 | bytes 2097152 | tf_op jit(solution)/shard_map/pallas_call | solution.py:322
  45.7 1.4 %copy.7 = bf16[2,3,32,64]{3,2,1,0:T(8,128)(2,1)} copy(bf16[2,3,32,64]{3,2,1,0:T(8,128)(2,1)} %shard_map.55) | data formatting | bytes 49152

commit v6 on v5

--- a/solution.py
+++ b/solution.py
@@ -84,16 +84,19 @@
         first = pl.multiple_of((peer % G) * C + starts[sub], LANES)
         return pltpu.make_async_remote_copy(
             src_ref=vectors.at[:, pl.ds(first, widths[sub])], dst_ref=gat[sub].at[me],
-            send_sem=send1.at[sub, k], recv_sem=recv1.at[sub, k],
+            send_sem=send1.at[sub], recv_sem=recv1.at[sub],
             device_id=(peer, place), device_id_type=MESH,
         )
 
     def norm_copy(k):
         return pltpu.make_async_remote_copy(
             src_ref=norm_src, dst_ref=norm_all.at[me],
-            send_sem=sendn.at[k], recv_sem=recvn.at[k],
+            send_sem=sendn, recv_sem=recvn,
             device_id=(peer_of(k), place), device_id_type=MESH,
         )
+
+    def drain(ref, sem):
+        pltpu.make_async_copy(ref, ref, sem).wait()
 
     def loop(count, step):
         def run(k, carry):
@@ -179,8 +182,8 @@
 
     def final_copy(g, k):
         return pltpu.make_async_remote_copy(
-            src_ref=final.at[g, k], dst_ref=recv.at[slot],
-            send_sem=send3.at[g, k], recv_sem=recv3.at[slot],
+            src_ref=final.at[g * per + k], dst_ref=recv.at[slot],
+            send_sem=send3, recv_sem=recv3,
             device_id=(base + index(g, k), place), device_id_type=MESH,
         )
 
@@ -204,12 +207,12 @@
                 whole = acc[g, k, core, place // 2] + mate_in[g, k, place // 2].astype(jnp.float32)
                 for lane in range(NF - 1):
                     whole = whole + cross_in[g, lane, k].astype(jnp.float32)
-                final[g, k] = whole.astype(final.dtype)
+                final[g * per + k] = whole.astype(final.dtype)
                 here = base + index(g, k) == me
 
                 @pl.when(here)
                 def _():
-                    pltpu.make_async_copy(final.at[g, k], recv.at[slot], recv3.at[slot]).start()
+                    pltpu.make_async_copy(final.at[g * per + k], recv.at[slot], recv3).start()
 
                 @pl.when(jnp.logical_not(here))
                 def _():
@@ -217,7 +220,7 @@
 
     for sub in range(subs):
         own_copy(sub).wait()
-        loop(N - 1, lambda k, sub=sub: block_copy(sub, k).wait_recv())
+        drain(gat[sub].at[pl.ds(0, N - 1)], recv1.at[sub])
         pivots(sub)
         if sub < subs - 1:
             def several(g, sub=sub):
@@ -240,7 +243,7 @@
         over_blk(groups - 2)
     over_blk(groups - 1)
 
-    loop(N - 1, lambda k: norm_copy(k).wait_recv())
+    drain(norm_all.at[pl.ds(0, N - 1)], recvn)
     lane = lax.broadcasted_iota(jnp.int32, (1, LANES), 1)
     line = lax.broadcasted_iota(jnp.int32, (share, LANES), 0)
     cols = lax.broadcasted_iota(jnp.int32, (share, LANES), 1)
@@ -259,14 +262,17 @@
 
     slots = G // 2
 
-    def arrived(k):
-        pltpu.make_async_remote_copy(
-            src_ref=final.at[0, 0], dst_ref=recv.at[k],
-            send_sem=send3.at[0, 0], recv_sem=recv3.at[k],
-            device_id=(mate, place), device_id_type=MESH,
-        ).wait_recv()
-
-    loop(slots, arrived)
+    for sub in range(subs):
+        drain(gat[sub].at[pl.ds(0, N - 1)], send1.at[sub])
+    drain(norm_all.at[pl.ds(0, N - 1)], sendn)
+    for g in range(groups):
+        mate_copy(g).wait_send()
+        for q in range(halves):
+            @pl.when(2 * q + core != place)
+            def _():
+                cross_copy(g, q).wait_send()
+
+    drain(recv, recv3)
     for s in range(npiv):
         whole = recv[0, s].astype(jnp.float32)
         for k in range(1, slots):
@@ -276,28 +282,9 @@
                 whole[:, t * rows : (t + 1) * rows] / divisors[t * npiv + s]
             ).astype(out.dtype)
 
-    for sub in range(subs):
-        loop(N - 1, lambda k, sub=sub: block_copy(sub, k).wait_send())
-    loop(N - 1, lambda k: norm_copy(k).wait_send())
-    for g in range(groups):
-        mate_copy(g).wait_send()
-
-    for g in range(groups):
-        for q in range(halves):
-            @pl.when(2 * q + core != place)
-            def _():
-                cross_copy(g, q).wait_send()
-
-    def sent(j):
-        g, k = j // per, j % per
-
-        @pl.when(base + index(g, k) != me)
-        def _():
-            final_copy(g, k).wait_send()
-
     @pl.when(gathers)
     def _():
-        loop(G, sent)
+        drain(final.at[pl.ds(0, G - 1)], send3)
 
 
 def body(vectors, norms, offsets, pivot_block, pivot_row):
@@ -306,8 +293,7 @@
     noff, npiv = pivot_block.shape
     G = min(N, fields // LANES)
     C = fields // G
-    tail = min(2, C // LANES - 1)
-    widths = (C - tail * LANES,) + (LANES,) * tail
+    widths = (C // 2, C // 2) if C % (2 * LANES) == 0 else (C,)
     groups = 4 if G % 4 == 0 else 1
     per = G // groups
     share = rows // NF
@@ -339,19 +325,19 @@
             pltpu.VMEM((groups, per, halves, npiv, share, wide), wire),
             pltpu.VMEM((groups, halves, per, npiv, share, wide), wire),
             pltpu.VMEM((groups, NF - 1, per, npiv, share, wide), wire),
-            pltpu.VMEM((groups, per, npiv, share, wide), wire),
+            pltpu.VMEM((G, npiv, share, wide), wire),
             pltpu.VMEM((slots, npiv, share, wide), wire),
-            dma((subs, N)),
-            dma((subs, N)),
             dma((subs,)),
-            dma((N,)),
-            dma((N,)),
+            dma((subs,)),
+            dma((subs,)),
+            dma,
+            dma,
             dma((groups,)),
             dma((groups,)),
             dma((groups, halves)),
             dma((groups, NF - 1)),
-            dma((groups, per)),
-            dma((slots,)),
+            dma,
+            dma,
         ],
         compiler_params=pltpu.CompilerParams(
             collective_id=0, has_side_effects=True, vmem_limit_bytes=63 * 1024 * 1024

time: 47.3 us -> 45.4 us (0.960)
  Pallas kernels: 45.7 us -> 43.8 us
    pallas_call x1, Pallas kernels: 45.7 us -> 43.8 us  [body(): pl.pallas_call(functools.partial(kernel, dims), out_shape=jax.ShapeDtypeS...]
where the time goes in v6:
time: 45.4 us; the launch traced here: 45.2 us
  Pallas kernels  43.8 us (96%)
  local copies, waits for them, and re-layouts  1.42 us (3%)
    pallas_call x1, Pallas kernels, body(): pl.pallas_call(functools.partial(kernel, dims), out_shape=jax.ShapeDtypeS...  43.8 us
    unnamed x1, local copies, waits for them, and re-layouts  1.42 us

profile of v6, /device:TPU:5, one launch (start us, length us, event | category | flops | bytes accessed | tf_op | source)
XLA Modules:
  0.0 45.2 jit_solution(9324067890350304072)
XLA Ops:
  0.0 43.8 %shard_map.55 = bf16[2,3,32,64]{3,2,1,0:T(8,128)(2,1)} custom-call(s32[2]{0:T(128)} %offsets_in.1, s32[2,3]{1,0:T(2,128)} %pivot_block_in.1, s32[2,3]{1,0:T(2,128)} %pivot_row_in.1, bf16[64,8192]{1,0:T(8,128)(2,1)} %vectors.1, bf16[1,64]{1,0:T(2,128)(2,1)} %bitcast.1), custom_call_target="tpu_custom_call" | custom-call | flops 402653184 | bytes 2097152 | tf_op jit(solution)/shard_map/pallas_call | solution.py:308
  43.8 1.4 %copy.7 = bf16[2,3,32,64]{3,2,1,0:T(8,128)(2,1)} copy(bf16[2,3,32,64]{3,2,1,0:T(8,128)(2,1)} %shard_map.55) | data formatting | bytes 49152

commit v7 on v6

--- a/solution.py
+++ b/solution.py
@@ -149,13 +149,22 @@
             value = jnp.where(
                 lane < t * rows, value, met[t * npiv * rows : (t + 1) * npiv * rows]
             )
+        pieces = {}
         for s in range(npiv):
             for h in range(NF):
                 first = s * rows + h * share
-                piece = value[first : first + share]
+                pieces[h % 2, h // 2, s] = value[first : first + share]
                 if sub > 0:
-                    piece = piece + acc[g, k, h % 2, h // 2, s]
-                acc[g, k, h % 2, h // 2, s] = piece
+                    pieces[h % 2, h // 2, s] += acc[g, k, h % 2, h // 2, s]
+        return pieces
+
+    def tiles(sub, g):
+        for first in range(0, per, 2):
+            pair = range(first, min(first + 2, per))
+            found = [tile(sub, g, k) for k in pair]
+            for k, pieces in zip(pair, found):
+                for (c, q, s), piece in pieces.items():
+                    acc[g, k, c, q, s] = piece
 
     def mate_copy(q):
         return pltpu.make_async_remote_copy(
@@ -224,13 +233,11 @@
         pivots(sub)
         if sub < subs - 1:
             def several(g, sub=sub):
-                for k in range(per):
-                    tile(sub, g, k)
+                tiles(sub, g)
 
             loop(groups, several)
     for g in range(groups):
-        for k in range(per):
-            tile(subs - 1, g, k)
+        tiles(subs - 1, g)
         for k in range(per):
             part[g, k] = acc[g, k, 1 - core].astype(part.dtype)
         mate_copy(g).start()

time: 45.4 us -> 45.4 us (level)
  no operation moved by 1% of the time
where the time goes in v7:
time: 45.4 us; the launch traced here: 45.2 us
  Pallas kernels  43.8 us (96%)
  local copies, waits for them, and re-layouts  1.42 us (3%)
    pallas_call x1, Pallas kernels, body(): pl.pallas_call(functools.partial(kernel, dims), out_shape=jax.ShapeDtypeS...  43.8 us
    unnamed x1, local copies, waits for them, and re-layouts  1.42 us

profile of v7, /device:TPU:5, one launch (start us, length us, event | category | flops | bytes accessed | tf_op | source)
XLA Modules:
  0.0 45.2 jit_solution(2831329568174113862)
XLA Ops:
  0.0 43.8 %shard_map.55 = bf16[2,3,32,64]{3,2,1,0:T(8,128)(2,1)} custom-call(s32[2]{0:T(128)} %offsets_in.1, s32[2,3]{1,0:T(2,128)} %pivot_block_in.1, s32[2,3]{1,0:T(2,128)} %pivot_row_in.1, bf16[64,8192]{1,0:T(8,128)(2,1)} %vectors.1, bf16[1,64]{1,0:T(2,128)(2,1)} %bitcast.1), custom_call_target="tpu_custom_call" | custom-call | flops 402653184 | bytes 2097152 | tf_op jit(solution)/shard_map/pallas_call | solution.py:315
  43.8 1.4 %copy.7 = bf16[2,3,32,64]{3,2,1,0:T(8,128)(2,1)} copy(bf16[2,3,32,64]{3,2,1,0:T(8,128)(2,1)} %shard_map.55) | data formatting | bytes 49152

commit v8 on v7

--- a/solution.py
+++ b/solution.py
@@ -300,7 +300,7 @@
     noff, npiv = pivot_block.shape
     G = min(N, fields // LANES)
     C = fields // G
-    widths = (C // 2, C // 2) if C % (2 * LANES) == 0 else (C,)
+    widths = (C,)
     groups = 4 if G % 4 == 0 else 1
     per = G // groups
     share = rows // NF

time: 45.4 us -> 45.6 us (level)
  no operation moved by 1% of the time
where the time goes in v8:
time: 45.6 us; the launch traced here: 45.4 us
  Pallas kernels  43.9 us (96%)
  local copies, waits for them, and re-layouts  1.42 us (3%)
    pallas_call x1, Pallas kernels, body(): pl.pallas_call(functools.partial(kernel, dims), out_shape=jax.ShapeDtypeS...  43.9 us
    unnamed x1, local copies, waits for them, and re-layouts  1.42 us

profile of v8, /device:TPU:5, one launch (start us, length us, event | category | flops | bytes accessed | tf_op | source)
XLA Modules:
  0.0 45.4 jit_solution(2019674926379437283)
XLA Ops:
  0.0 43.9 %shard_map.55 = bf16[2,3,32,64]{3,2,1,0:T(8,128)(2,1)} custom-call(s32[2]{0:T(128)} %offsets_in.1, s32[2,3]{1,0:T(2,128)} %pivot_block_in.1, s32[2,3]{1,0:T(2,128)} %pivot_row_in.1, bf16[64,8192]{1,0:T(8,128)(2,1)} %vectors.1, bf16[1,64]{1,0:T(2,128)(2,1)} %bitcast.1), custom_call_target="tpu_custom_call" | custom-call | flops 402653184 | bytes 2097152 | tf_op jit(solution)/shard_map/pallas_call | solution.py:315
  44.0 1.4 %copy.7 = bf16[2,3,32,64]{3,2,1,0:T(8,128)(2,1)} copy(bf16[2,3,32,64]{3,2,1,0:T(8,128)(2,1)} %shard_map.55) | data formatting | bytes 49152

commit v9 on v7

--- a/solution.py
+++ b/solution.py
@@ -13,8 +13,8 @@
 
 def kernel(
     dims, offsets_in, pivot_block_in, pivot_row_in, vectors, norms_in, out,
-    offsets, pivot_block, pivot_row, norms, small, gat, norm_src, norm_all, piv, acc, part, mate_in, total, cross_in, final, recv,
-    send1, recv1, own1, sendn, recvn, send2, recv2, sendx, recvx, send3, recv3,
+    offsets, pivot_block, pivot_row, norms, small, gat, norm_src, norm_all, piv, acc, part, mate_in, total, recv,
+    send1, recv1, own1, sendn, recvn, send2, recv2, send3, recv3,
 ):
     N, NF, G, C, widths, groups, rows, noff, npiv = dims
     share = rows // NF
@@ -27,7 +27,7 @@
     base = group * G
     core = me % 2
     mate = me + 1 - 2 * core
-    slot = chunk // 2
+    slot = (chunk // 2) * NF + place
     gathers = place % 2 == core
 
     barrier = pltpu.get_barrier_semaphore()
@@ -39,13 +39,14 @@
         return carry
 
     def greet_fld(j, carry):
+        other = lax.rem(place + 1 + j // G, NF)
         pl.semaphore_signal(
-            barrier, inc=1, device_id=(me, lax.rem(place + j, NF)), device_id_type=MESH
+            barrier, inc=1, device_id=(base + j % G, other), device_id_type=MESH
         )
         return carry
 
     lax.fori_loop(1, N, greet_blk, 0)
-    lax.fori_loop(1, NF, greet_fld, 0)
+    lax.fori_loop(0, G * (NF - 1), greet_fld, 0)
 
     smalls = [
         pltpu.make_async_copy(src, dst, small.at[k])
@@ -69,7 +70,7 @@
     smalls[0].wait()
     norm_src[0:1, 0:rows] = norms[...].astype(jnp.float32)
     norm_all[me] = norm_src[...]
-    pl.semaphore_wait(barrier, (N - 1) + (NF - 1))
+    pl.semaphore_wait(barrier, (N - 1) + G * (NF - 1))
 
     side = N // 2
 
@@ -173,59 +174,30 @@
             device_id=(mate, place), device_id_type=MESH,
         )
 
-    def cross_copy(g, q):
-        target = 2 * q + core
-        lane = lax.rem(place - target + NF, NF) - 1
+    def total_copy(g, k, q):
         return pltpu.make_async_remote_copy(
-            src_ref=total.at[g, q], dst_ref=cross_in.at[g, lane],
-            send_sem=sendx.at[g, q], recv_sem=recvx.at[g, lane],
-            device_id=(me, target), device_id_type=MESH,
-        )
-
-    def cross_arrival(g, lane):
-        return pltpu.make_async_remote_copy(
-            src_ref=total.at[g, 0], dst_ref=cross_in.at[g, lane],
-            send_sem=sendx.at[g, 0], recv_sem=recvx.at[g, lane],
-            device_id=(me, lax.rem(place + 1, NF)), device_id_type=MESH,
-        )
-
-    def final_copy(g, k):
-        return pltpu.make_async_remote_copy(
-            src_ref=final.at[g * per + k], dst_ref=recv.at[slot],
+            src_ref=total.at[(g * per + k) * halves + q], dst_ref=recv.at[slot],
             send_sem=send3, recv_sem=recv3,
-            device_id=(base + index(g, k), place), device_id_type=MESH,
-        )
-
-    def over_fld(g):
+            device_id=(base + index(g, k), 2 * q + core), device_id_type=MESH,
+        )
+
+    def hand_out(g):
         mate_copy(g).wait_recv()
-        for q in range(halves):
-            @pl.when(2 * q + core != place)
-            def _():
-                for k in range(per):
-                    total[g, q, k] = (
-                        acc[g, k, core, q] + mate_in[g, k, q].astype(jnp.float32)
-                    ).astype(total.dtype)
-                cross_copy(g, q).start()
-
-    def over_blk(g):
-        @pl.when(gathers)
-        def _():
-            for lane in range(NF - 1):
-                cross_arrival(g, lane).wait_recv()
-            for k in range(per):
-                whole = acc[g, k, core, place // 2] + mate_in[g, k, place // 2].astype(jnp.float32)
-                for lane in range(NF - 1):
-                    whole = whole + cross_in[g, lane, k].astype(jnp.float32)
-                final[g * per + k] = whole.astype(final.dtype)
-                here = base + index(g, k) == me
+        for k in range(per):
+            for q in range(halves):
+                spot = (g * per + k) * halves + q
+                total[spot] = (
+                    acc[g, k, core, q] + mate_in[g, k, q].astype(jnp.float32)
+                ).astype(total.dtype)
+                here = jnp.logical_and(base + index(g, k) == me, 2 * q + core == place)
 
                 @pl.when(here)
                 def _():
-                    pltpu.make_async_copy(final.at[g * per + k], recv.at[slot], recv3).start()
+                    pltpu.make_async_copy(total.at[spot], recv.at[slot], recv3).start()
 
                 @pl.when(jnp.logical_not(here))
                 def _():
-                    final_copy(g, k).start()
+                    total_copy(g, k, q).start()
 
     for sub in range(subs):
         own_copy(sub).wait()
@@ -242,13 +214,8 @@
             part[g, k] = acc[g, k, 1 - core].astype(part.dtype)
         mate_copy(g).start()
         if g > 0:
-            over_fld(g - 1)
-        if g > 1:
-            over_blk(g - 2)
-    over_fld(groups - 1)
-    if groups > 1:
-        over_blk(groups - 2)
-    over_blk(groups - 1)
+            hand_out(g - 1)
+    hand_out(groups - 1)
 
     drain(norm_all.at[pl.ds(0, N - 1)], recvn)
     lane = lax.broadcasted_iota(jnp.int32, (1, LANES), 1)
@@ -267,17 +234,13 @@
             )
             divisors.append((own_norms * pivot_norm) * partner_norms[t])
 
-    slots = G // 2
+    slots = (G // 2) * NF
 
     for sub in range(subs):
         drain(gat[sub].at[pl.ds(0, N - 1)], send1.at[sub])
     drain(norm_all.at[pl.ds(0, N - 1)], sendn)
     for g in range(groups):
         mate_copy(g).wait_send()
-        for q in range(halves):
-            @pl.when(2 * q + core != place)
-            def _():
-                cross_copy(g, q).wait_send()
 
     drain(recv, recv3)
     for s in range(npiv):
@@ -291,7 +254,11 @@
 
     @pl.when(gathers)
     def _():
-        drain(final.at[pl.ds(0, G - 1)], send3)
+        drain(total.at[pl.ds(0, G * halves - 1)], send3)
+
+    @pl.when(jnp.logical_not(gathers))
+    def _():
+        drain(total, send3)
 
 
 def body(vectors, norms, offsets, pivot_block, pivot_row):
@@ -307,7 +274,7 @@
     halves = NF // 2
     wire = jnp.bfloat16 if share % 16 == 0 else jnp.float32
     wide = noff * rows
-    slots = G // 2
+    slots = (G // 2) * NF
     subs = len(widths)
     dims = (N, NF, G, C, widths, groups, rows, noff, npiv)
     dma = pltpu.SemaphoreType.DMA
@@ -330,9 +297,7 @@
             pltpu.VMEM((groups, per, 2, halves, npiv, share, wide), jnp.float32),
             pltpu.VMEM((groups, per, halves, npiv, share, wide), wire),
             pltpu.VMEM((groups, per, halves, npiv, share, wide), wire),
-            pltpu.VMEM((groups, halves, per, npiv, share, wide), wire),
-            pltpu.VMEM((groups, NF - 1, per, npiv, share, wide), wire),
-            pltpu.VMEM((G, npiv, share, wide), wire),
+            pltpu.VMEM((G * halves, npiv, share, wide), wire),
             pltpu.VMEM((slots, npiv, share, wide), wire),
             dma((subs,)),
             dma((subs,)),
@@ -341,8 +306,6 @@
             dma,
             dma((groups,)),
             dma((groups,)),
-            dma((groups, halves)),
-            dma((groups, NF - 1)),
             dma,
             dma,
         ],

time: 45.4 us -> 45 us (level); the launches traced: 45.2 us -> 44.3 us
  Pallas kernels: 43.8 us -> 42.9 us
    pallas_call x1, Pallas kernels: 43.8 us -> 42.9 us  [body(): pl.pallas_call(functools.partial(kernel, dims), out_shape=jax.ShapeDtypeS...]
where the time goes in v9:
time: 45 us; the launch traced here: 44.3 us
  Pallas kernels  42.9 us (95%)
  local copies, waits for them, and re-layouts  1.42 us (3%)
    pallas_call x1, Pallas kernels, body(): pl.pallas_call(functools.partial(kernel, dims), out_shape=jax.ShapeDtypeS...  42.9 us
    unnamed x1, local copies, waits for them, and re-layouts  1.42 us

profile of v9, /device:TPU:5, one launch (start us, length us, event | category | flops | bytes accessed | tf_op | source)
XLA Modules:
  0.0 44.3 jit_solution(6694031271564331439)
XLA Ops:
  0.0 42.9 %shard_map.55 = bf16[2,3,32,64]{3,2,1,0:T(8,128)(2,1)} custom-call(s32[2]{0:T(128)} %offsets_in.1, s32[2,3]{1,0:T(2,128)} %pivot_block_in.1, s32[2,3]{1,0:T(2,128)} %pivot_row_in.1, bf16[64,8192]{1,0:T(8,128)(2,1)} %vectors.1, bf16[1,64]{1,0:T(2,128)(2,1)} %bitcast.1), custom_call_target="tpu_custom_call" | custom-call | flops 402653184 | bytes 2097152 | tf_op jit(solution)/shard_map/pallas_call | solution.py:282
  42.9 1.4 %copy.7 = bf16[2,3,32,64]{3,2,1,0:T(8,128)(2,1)} copy(bf16[2,3,32,64]{3,2,1,0:T(8,128)(2,1)} %shard_map.55) | data formatting | bytes 49152

commit v10 on v9

--- a/solution.py
+++ b/solution.py
@@ -32,21 +32,15 @@
 
     barrier = pltpu.get_barrier_semaphore()
 
-    def greet_blk(j, carry):
+    for j in range(1, N):
         pl.semaphore_signal(
             barrier, inc=1, device_id=(lax.rem(me + j, N), place), device_id_type=MESH
         )
-        return carry
-
-    def greet_fld(j, carry):
-        other = lax.rem(place + 1 + j // G, NF)
-        pl.semaphore_signal(
-            barrier, inc=1, device_id=(base + j % G, other), device_id_type=MESH
-        )
-        return carry
-
-    lax.fori_loop(1, N, greet_blk, 0)
-    lax.fori_loop(0, G * (NF - 1), greet_fld, 0)
+    for f in range(1, NF):
+        for j in range(G):
+            pl.semaphore_signal(
+                barrier, inc=1, device_id=(base + j, lax.rem(place + f, NF)), device_id_type=MESH
+            )
 
     smalls = [
         pltpu.make_async_copy(src, dst, small.at[k])
@@ -76,9 +70,8 @@
 
     def peer_of(k):
         half, spot = me // side, me % side
-        other = k % 2 == 0
         turn = lax.rem(spot + (k + 1) // 2, side)
-        return jnp.where(other, 1 - half, half) * side + turn
+        return (1 - half if k % 2 == 0 else half) * side + turn
 
     def block_copy(sub, k):
         peer = peer_of(k)
@@ -107,8 +100,10 @@
         lax.fori_loop(0, count, run, 0)
 
     for sub in range(subs):
-        loop(N - 1, lambda k, sub=sub: block_copy(sub, k).start())
-    loop(N - 1, lambda k: norm_copy(k).start())
+        for k in range(N - 1):
+            block_copy(sub, k).start()
+    for k in range(N - 1):
+        norm_copy(k).start()
 
     for copy in smalls[1:]:
         copy.wait()

time: 45 us -> 44.9 us (level)
  no operation moved by 1% of the time
where the time goes in v10:
time: 44.9 us; the launch traced here: 44.2 us
  Pallas kernels  42.8 us (95%)
  local copies, waits for them, and re-layouts  1.42 us (3%)
    pallas_call x1, Pallas kernels, body(): pl.pallas_call(functools.partial(kernel, dims), out_shape=jax.ShapeDtypeS...  42.8 us
    unnamed x1, local copies, waits for them, and re-layouts  1.42 us

profile of v10, /device:TPU:5, one launch (start us, length us, event | category | flops | bytes accessed | tf_op | source)
XLA Modules:
  0.0 44.2 jit_solution(9594282845747521421)
XLA Ops:
  0.0 42.8 %shard_map.55 = bf16[2,3,32,64]{3,2,1,0:T(8,128)(2,1)} custom-call(s32[2]{0:T(128)} %offsets_in.1, s32[2,3]{1,0:T(2,128)} %pivot_block_in.1, s32[2,3]{1,0:T(2,128)} %pivot_row_in.1, bf16[64,8192]{1,0:T(8,128)(2,1)} %vectors.1, bf16[1,64]{1,0:T(2,128)(2,1)} %bitcast.1), custom_call_target="tpu_custom_call" | custom-call | flops 402653184 | bytes 2097152 | tf_op jit(solution)/shard_map/pallas_call | solution.py:277
  42.8 1.4 %copy.7 = bf16[2,3,32,64]{3,2,1,0:T(8,128)(2,1)} copy(bf16[2,3,32,64]{3,2,1,0:T(8,128)(2,1)} %shard_map.55) | data formatting | bytes 49152
